TPU v7x, 32 devices: a whole 2x2x4 slice. The times are simulated.
32 devices in a mesh: ab: 4 (over y, x), cd: 8 (over z, core).
Axes of the slice: x: 2, y: 2, z: 4, core: 2. Of those that a mesh axis runs over, the one named last changes fastest.
Arguments:
- factors: bfloat16 [128, 128, 2048], P('ab', 'cd'), may hold values from -0.25 to 0.25
- amplitudes: float32 [256, 128, 128], P('cd', 'ab'), may hold values from -4 to 4
- driving: float32 [256, 128, 128], P('cd', 'ab'), may hold values from -8 to 8
- occ_energy: float32 [32], replicated, may hold values from -2 to -0.5
- vir_energy: float32 [128], replicated, may hold values from 0.5 to 3
Outputs:
- new_amplitudes: float32 [256, 128, 128], P('cd', 'ab')
- residual: float32 [256, 128, 128], P('cd', 'ab')
All inputs are finite; a program needn't handle non-finite values.
Results may differ from a plain program's by a relative error of at most 0.0036.
Values may be sent and summed in bfloat16 or wider, within the bound.
A program may use at most 128 MiB of HBM per device.

v0:
```python
import jax
import jax.numpy as jnp
from jax import lax
from jax.sharding import PartitionSpec as P

ITERS = 2


def local(factors, amplitudes, driving, occ_energy, vir_energy):
    rows = amplitudes.shape[0]
    a_local = amplitudes.shape[1]
    virtuals = amplitudes.shape[2]
    aux_width = factors.shape[2]
    n_cd = lax.axis_size("cd")
    d_local = factors.shape[1]
    pairs = rows * n_cd
    cd_index = lax.axis_index("cd")
    ab_index = lax.axis_index("ab")
    left_rows = lax.all_gather(factors, "cd", axis=1, tiled=True)
    left_flat = left_rows.reshape(a_local * virtuals, aux_width)
    piece = lax.all_gather(factors, "ab", axis=0, tiled=True)
    count = piece.shape[0]
    product = lax.dot_general(
        left_flat,
        piece.reshape(count * d_local, aux_width),
        (((1,), (1,)), ((), ())),
        preferred_element_type=jnp.float32,
    )
    product = product.reshape(a_local, virtuals, count, d_local)
    tiles = (
        product.transpose(0, 2, 3, 1)
        .reshape(a_local, count, d_local * virtuals)
        .astype(jnp.bfloat16)
    )
    tiles = tiles.reshape(a_local * virtuals, d_local * virtuals)
    n_occ = occ_energy.shape[0]
    row_ids = cd_index * rows + lax.iota(jnp.int32, rows)
    orbitals = lax.iota(jnp.int32, n_occ)
    first_hot = (row_ids[:, None] // n_occ == orbitals[None, :]).astype(jnp.float32)
    second_hot = (row_ids[:, None] % n_occ == orbitals[None, :]).astype(jnp.float32)
    occ_pair = jnp.sum((first_hot + second_hot) * occ_energy[None, :], axis=1)
    vir_rows = lax.dynamic_slice_in_dim(vir_energy, ab_index * a_local, a_local)
    denominator = vir_rows[None, :, None] + vir_energy[None, None, :] - occ_pair[:, None, None]
    current = amplitudes
    residual = amplitudes
    for step in range(ITERS):
        rounded = current.astype(jnp.bfloat16)
        own_block = lax.all_to_all(
            rounded.transpose(2, 1, 0), "cd", split_axis=0, concat_axis=2, tiled=True
        )
        gathered = lax.all_gather(own_block, "ab", axis=1, tiled=True)
        flat_amps = gathered.reshape(d_local * virtuals, pairs)
        summed = lax.psum_scatter(
            lax.dot_general(
                flat_amps, tiles, (((0,), (1,)), ((), ())), preferred_element_type=jnp.float32
            ),
            "cd",
            scatter_dimension=0,
            tiled=True,
        ).reshape(rows, a_local, virtuals)
        mirrored = lax.all_to_all(summed, "ab", split_axis=2, concat_axis=1, tiled=True).transpose(
            0, 2, 1
        )
        symmetric = 0.5 * (summed + mirrored)
        residual = driving + denominator * current + symmetric
        current = current - residual / denominator
    return (current, residual)


def solution(mesh):
    placed = (P("ab", "cd", None), P("cd", "ab", None), P("cd", "ab", None), P(), P())
    return jax.shard_map(
        local,
        mesh=mesh,
        in_specs=placed,
        out_specs=(P("cd", "ab", None), P("cd", "ab", None)),
        check_vma=False,
    )
```

profile of v0, /device:TPU:22, one launch (start us, length us, event | category | flops | bytes accessed | tf_op | source)
XLA Modules:
  0.0 550.3 jit_solution(2896369535168366662)
XLA Ops:
  7.2 0.0 copy-start
  7.2 0.0 all-gather.7.cloned.1.call-start
  7.2 4.1 copy.88
  11.3 0.0 all-gather.7.cloned.1.call-update
  11.4 0.0 all-gather.5.cloned.1.call-start
  11.4 0.7 all-gather.5.cloned.1.call-update
  12.1 0.0 all-gather.9.cloned.1.call-start
  12.2 0.0 copy-done
  12.2 1.4 copy.90
  13.7 1.0 reshape.126
  14.6 11.4 %all_to_all.72 = bf16[8,2,8192]{2,1,0:T(2,128)(2,1)S(1)} all-to-all(bf16[8,2,8192]{2,1,0:T(2,128)(2,1)S(1)} %reshape.126), channel_id=1, replica_groups=mesh['ab'=4,'cd'=8] {'cd'}, dimensions={0} | all-to-all | bytes 524288 | tf_op jit(solution)/shard_map/all_to_all | solution.py:48
  26.1 0.5 reshape.127
  26.6 0.8 copy.92
  27.4 1.4 all_to_all.55
  28.8 0.0 all-gather.9.cloned.1.call-update
  28.8 0.2 reduce-scatter.7.cloned.1.call-start
  29.1 70.1 %all-gather.7.cloned.1.call-done = bf16[128,16,2048]{2,0,1:T(8,128)(2,1)} async-done(((bf16[32,16,2048]{2,0,1:T(8,128)(2,1)}), bf16[128,16,2048]{2,0,1:T(8,128)(2,1)}) %all-gather.7.cloned.1.call-update) | async-done | bytes 8388624 | tf_op jit(solution)/shard_map/all_gather | solution.py:21
  99.2 151.9 %all-gather.5.cloned.1.call-done = bf16[32,128,2048]{2,1,0:T(8,128)(2,1)} async-done(((bf16[32,16,2048]{2,1,0:T(8,128)(2,1)}), bf16[32,128,2048]{2,1,0:T(8,128)(2,1)}) %all-gather.5.cloned.1.call-update) | async-done | bytes 16777232 | tf_op jit(solution)/shard_map/all_gather | solution.py:19
  251.1 41.3 %convert_bitcast_fusion = bf16[32,128,16,128]{1,3,2,0:T(8,128)(2,1)} fusion(bf16[32,128,2048]{2,1,0:T(8,128)(2,1)} %all-gather.5.cloned.1.call-done, bf16[128,16,2048]{2,0,1:T(8,128)(2,1)} %all-gather.7.cloned.1.call-done), kind=kOutput, calls=%fused_computation.6 | convolution fusion | flops 34368126976 | bytes 41943040 | tf_op jit(solution)/shard_map/dot_general | solution.py:23
  292.4 22.4 %copy.89 = bf16[32,128,16,128]{3,2,1,0:T(8,128)(2,1)} copy(bf16[32,128,16,128]{1,3,2,0:T(8,128)(2,1)} %convert_bitcast_fusion) | data formatting | bytes 33554432 | tf_op jit(solution)/shard_map/convert_element_type | solution.py:33
  314.7 12.8 %fusion.11 = f32[256,4096]{0,1:T(8,128)} fusion(bf16[2048,256]{1,0:T(8,128)(2,1)} %bitcast.97, bf16[512,8,16,128]{3,2,1,0:T(8,128)(2,1)} %bitcast.83), kind=kOutput, calls=%fused_computation.10 | convolution fusion | flops 4294967296 | bytes 22020096 | tf_op jit(solution)/shard_map/dot_general | solution.py:54
  327.5 5.6 %copy.106 = f32[256,4096]{1,0:T(8,128)} copy(f32[256,4096]{0,1:T(8,128)} %fusion.11) | data formatting | bytes 8388608
  333.1 0.0 reduce-scatter.7.cloned.1.call-update
  333.1 46.7 %reduce-scatter.7.cloned.1.call-done = f32[32,4096]{1,0:T(8,128)} async-done(((f32[256,4096]{1,0:T(8,128)}), f32[32,4096]{1,0:T(8,128)}) %reduce-scatter.7.cloned.1.call-update) | async-done | bytes 524304
  379.9 1.6 copy.107
  381.5 2.6 copy.123
  384.1 2.9 reshape.128
  387.0 5.5 all-to-all-start.1
  392.5 0.2 all-gather.11.cloned.1.call-start
  392.7 0.0 copy-done.2
  392.7 0.1 dynamic_slice.3
  392.8 0.0 copy-done.3
  392.8 0.2 multiply_reduce_fusion
  393.0 0.1 broadcast_add_fusion
  393.0 0.7 copy.103
  393.8 6.5 %all-to-all-done.1 = f32[4,1,32768]{2,1,0:T(1,128)} async-done(((f32[4,1,32768]{2,1,0:T(1,128)}), f32[4,1,32768]{2,1,0:T(1,128)}, u32[]{:S(2)}, u32[]{:S(2)}) %all-to-all-start.1) | async-done | bytes 524320 | tf_op jit(solution)/shard_map/all_to_all | solution.py:61
  400.3 0.5 broadcast.119
  400.8 3.8 reduce
  404.7 1.8 reshape.129
  406.4 2.7 copy.95
  409.1 2.4 all_to_all.59
  411.5 0.0 copy-done.1
  411.5 2.1 convert_bitcast_fusion.1
  413.6 1.4 copy.96
  415.0 1.0 reshape.130
  416.0 10.4 %all_to_all.73 = bf16[8,2,8192]{2,1,0:T(2,128)(2,1)S(1)} all-to-all(bf16[8,2,8192]{2,1,0:T(2,128)(2,1)S(1)} %reshape.130), channel_id=1, replica_groups=mesh['ab'=4,'cd'=8] {'cd'}, dimensions={0} | all-to-all | bytes 524288 | tf_op jit(solution)/shard_map/all_to_all | solution.py:48
  426.4 0.5 reshape.131
  426.9 0.8 copy.98
  427.7 1.4 all_to_all.63
  429.2 0.0 all-gather.11.cloned.1.call-update
  429.2 0.3 reduce-scatter.5.cloned.1.call-start
  429.5 27.3 %all-gather.11.cloned.1.call-done = bf16[16,128,256]{2,1,0:T(8,128)(2,1)} async-done(((bf16[16,32,256]{2,1,0:T(8,128)(2,1)}), bf16[16,128,256]{2,1,0:T(8,128)(2,1)}) %all-gather.11.cloned.1.call-update) | async-done | bytes 1048592 | tf_op jit(solution)/shard_map/all_gather | solution.py:51
  456.8 12.6 %fusion = f32[256,4096]{1,0:T(8,128)} fusion(bf16[2048,256]{1,0:T(8,128)(2,1)} %bitcast.98, bf16[512,8,16,128]{3,2,1,0:T(8,128)(2,1)} %bitcast.84), kind=kOutput, calls=%fused_computation | convolution fusion | flops 4294967296 | bytes 22020096 | tf_op jit(solution)/shard_map/dot_general | solution.py:54
  469.4 0.0 reduce-scatter.5.cloned.1.call-update
  469.4 47.7 %reduce-scatter.5.cloned.1.call-done = f32[32,4096]{1,0:T(8,128)} async-done(((f32[256,4096]{1,0:T(8,128)}), f32[32,4096]{1,0:T(8,128)}) %reduce-scatter.5.cloned.1.call-update) | async-done | bytes 524304 | tf_op jit(solution)/shard_map/reduce_scatter | solution.py:53
  517.2 1.1 copy.109
  518.3 1.8 copy.99
  520.1 0.9 reshape.132
  521.1 11.5 %all_to_all.74 = f32[4,1,32768]{2,1,0:T(1,128)S(1)} all-to-all(f32[4,1,32768]{2,1,0:T(1,128)S(1)} %reshape.132), channel_id=1, replica_groups=mesh['ab'=4,'cd'=8] {'ab'}, dimensions={0} | all-to-all | bytes 1048576 | tf_op jit(solution)/shard_map/all_to_all | solution.py:61
  532.6 2.1 reduce.1
  534.8 0.7 reshape.133
  535.5 2.7 copy.122
  538.2 2.4 all_to_all.67
  540.6 2.4 fusion.19
  (6 shorter events, 0.1 us)
Async XLA Ops:
  7.2 5.0 copy-start
  7.2 92.0 %all-gather.7.cloned.1.call-start = ((), (), s32[]{:S(2)}) async-start(), calls=%async_computation.7 | async-start | bytes 10485760 | tf_op jit(solution)/shard_map/all_gather | solution.py:21
  11.4 239.7 %all-gather.5.cloned.1.call-start = ((), (), s32[]{:S(2)}) async-start(), calls=%async_computation.6 | async-start | bytes 18874368 | tf_op jit(solution)/shard_map/all_gather | solution.py:19
  12.1 302.6 %all-gather.9.cloned.1.call-start = ((), (), s32[]{:S(2)}) async-start(), calls=%async_computation.8 | async-start | bytes 1310720 | tf_op jit(solution)/shard_map/all_gather | solution.py:51
  28.8 351.0 %reduce-scatter.7.cloned.1.call-start = ((), (), s32[]{:S(2)}) async-start(), calls=%async_computation.11 | async-start | bytes 4718592
  333.1 59.6 %copy-start.2 = (f32[128]{0:T(128)S(1)}, f32[128]{0:T(128)}, u32[]{:S(2)}) copy-start(f32[128]{0:T(128)} %param.9) | copy-start | bytes 1540
  333.1 59.7 %copy-start.3 = (f32[32]{0:T(128)S(1)}, f32[32]{0:T(128)}, u32[]{:S(2)}) copy-start(f32[32]{0:T(128)} %param.8) | copy-start | bytes 388
  384.1 27.4 %copy-start.1 = (f32[32,32,128]{2,1,0:T(8,128)S(1)}, f32[32,32,128]{2,1,0:T(8,128)}, u32[]{:S(2)}) copy-start(f32[32,32,128]{2,1,0:T(8,128)} %param.6) | copy-start | bytes 1572868
  387.0 13.3 %all-to-all-start.1 = ((f32[4,1,32768]{2,1,0:T(1,128)}), f32[4,1,32768]{2,1,0:T(1,128)}, u32[]{:S(2)}, u32[]{:S(2)}) async-start(f32[4,1,32768]{2,1,0:T(1,128)} %reshape.128), calls=%async_computation.1 | async-start | bytes 1048576 | tf_op jit(solution)/shard_map/all_to_all | solution.py:61
  392.5 64.3 %all-gather.11.cloned.1.call-start = ((), (), s32[]{:S(2)}) async-start(), calls=%async_computation.9 | async-start | bytes 1310720 | tf_op jit(solution)/shard_map/all_gather | solution.py:51
  429.2 88.0 %reduce-scatter.5.cloned.1.call-start = ((), (), s32[]{:S(2)}) async-start(), calls=%async_computation.10 | async-start | bytes 4718592 | tf_op jit(solution)/shard_map/reduce_scatter | solution.py:53
Sparse Core Ops, SparseCore 0:
  11.5 87.6 all-gather.6
  100.8 150.2 all-gather.4
  253.5 25.6 all-gather.8
  333.2 46.5 reduce-scatter.6
  429.3 27.3 all-gather.10
  469.5 47.5 reduce-scatter.4
where the time goes:
time: 560 us; the launch traced here: 550 us
  waiting for transfers between devices  351 us (63%)
  local copies, waits for them, and re-layouts  67.4 us (12%)
  matrix products  66.7 us (12%)
  blocking collectives  33.4 us (6%)
  between operations  14.7 us (3%)
  other arithmetic  10.7 us (2%)
  starting transfers between devices  6.32 us (1%)
    all_gather x1, waiting for transfers between devices, local(): left_rows = lax.all_gather(factors, 'cd', axis=1, tiled=True)  152 us
    all_gather x1, waiting for transfers between devices, local(): piece = lax.all_gather(factors, 'ab', axis=0, tiled=True)  70.1 us
    reduce_scatter x1, waiting for transfers between devices, local(): lax.psum_scatter(lax.dot_general(flat_amps, tiles, (((0,), (1,)), ((), ()...  47.7 us
    unnamed x7, waiting for transfers between devices  47.5 us
    dot_general x1, matrix products, local(): lax.dot_general(left_flat, piece.reshape(count * d_local, aux_width), (((...  41.3 us
    all_gather x2, waiting for transfers between devices, local(): gathered = lax.all_gather(own_block, 'ab', axis=1, tiled=True)  27.3 us
    dot_general x2, matrix products, local(): lax.dot_general(flat_amps, tiles, (((0,), (1,)), ((), ())), preferred_ele...  25.4 us
    convert_element_type x1, local copies, waits for them, and re-layouts, local(): tiles = product.transpose(0, 2, 3, 1).reshape(a_local, count, d_local * v...  22.4 us
  transfers between devices with their start and end apart: 7, of which 6 were waited for; matrix products, arithmetic and copies ran while one was open for 12% of the time, Pallas kernels for 0%

commit v1 on v0

--- a/solution.py
+++ b/solution.py
@@ -1,12 +1,17 @@
+import functools
+
 import jax
 import jax.numpy as jnp
 from jax import lax
+from jax.experimental import pallas as pl
+from jax.experimental.pallas import tpu as pltpu
 from jax.sharding import PartitionSpec as P
 
 ITERS = 2
-
-
-def local(factors, amplitudes, driving, occ_energy, vir_energy):
+MESH = pl.DeviceIdType.MESH
+
+
+def local_general(factors, amplitudes, driving, occ_energy, vir_energy):
     rows = amplitudes.shape[0]
     a_local = amplitudes.shape[1]
     virtuals = amplitudes.shape[2]
@@ -67,8 +72,261 @@
     return (current, residual)
 
 
+def integral_kernel(virtuals, d_local, left_ref, right_ref, out_ref):
+    a_step = left_ref.shape[0] // virtuals
+    product = lax.dot_general(
+        left_ref[...], right_ref[...], (((1,), (1,)), ((), ())), preferred_element_type=jnp.float32
+    ).astype(jnp.bfloat16)
+    for a in range(a_step):
+        for d in range(d_local):
+            out_ref[d * virtuals:(d + 1) * virtuals, a * virtuals:(a + 1) * virtuals] = product[
+                a * virtuals:(a + 1) * virtuals, d * virtuals:(d + 1) * virtuals
+            ]
+
+
+def integral_tiles(left, right, virtuals, d_local):
+    a_step = 2
+    rows, depth = left.shape
+    a_local = rows // virtuals
+    return pl.pallas_call(
+        functools.partial(integral_kernel, virtuals, d_local),
+        grid=(a_local // a_step,),
+        in_specs=[
+            pl.BlockSpec((a_step * virtuals, depth), lambda i: (i, 0)),
+            pl.BlockSpec(right.shape, lambda i: (0, 0)),
+        ],
+        out_specs=pl.BlockSpec((d_local * virtuals, a_step * virtuals), lambda i: (0, i)),
+        out_shape=jax.ShapeDtypeStruct((d_local * virtuals, a_local * virtuals), jnp.bfloat16),
+        compiler_params=pltpu.CompilerParams(vmem_limit_bytes=48 * 2**20),
+        cost_estimate=pl.CostEstimate(
+            flops=2 * rows * right.shape[0] * depth,
+            bytes_accessed=2 * (rows * depth + right.size + rows * right.shape[0]),
+            transcendentals=0,
+        ),
+    )(left, right)
+
+
+def ladder_kernel(
+    n_ab, n_cd, chunks, v_ref, sym_amp_ref, sym_drv_ref, den_ref, out_ref,
+    amps, part, pair_in, pair_out, arrived, state, packed,
+    amp_send, amp_recv, amp_local, pair_send, pair_recv, red_send, red_recv,
+):
+    ab = lax.axis_index("ab")
+    cd = lax.axis_index("cd")
+    n_z = n_cd // 2
+    z = cd // 2
+    h = cd % 2
+    rows, width = sym_amp_ref.shape
+    depth = v_ref.shape[0]
+    cols = width // chunks
+
+    barrier = pltpu.get_barrier_semaphore()
+    for i in range(n_ab):
+        for j in range(n_cd):
+            @pl.when(jnp.logical_not((ab == i) & (cd == j)))
+            def _():
+                pl.semaphore_signal(barrier, inc=1, device_id=(i, j), device_id_type=MESH)
+    pl.semaphore_wait(barrier, n_ab * n_cd - 1)
+
+    state[...] = sym_amp_ref[...]
+
+    def amp_copy(it, i, k):
+        return pltpu.make_async_remote_copy(
+            src_ref=packed.at[it, :, pl.ds(k * depth, depth)],
+            dst_ref=amps.at[it, pl.ds(cd * rows, rows), :],
+            send_sem=amp_send.at[it, i, k],
+            recv_sem=amp_recv.at[it, cd],
+            device_id=(i, 2 * ab + k),
+            device_id_type=MESH,
+        )
+
+    def amp_local_copy(it, k):
+        return pltpu.make_async_copy(
+            packed.at[it, :, pl.ds(k * depth, depth)],
+            amps.at[it, pl.ds(cd * rows, rows), :],
+            amp_local.at[it],
+        )
+
+    def amp_arrival(it, j):
+        return pltpu.make_async_remote_copy(
+            src_ref=packed.at[it, :, pl.ds(0, depth)],
+            dst_ref=amps.at[it, pl.ds(j * rows, rows), :],
+            send_sem=amp_send.at[it, 0, 0],
+            recv_sem=amp_recv.at[it, j],
+            device_id=(ab, 1 - h + 2 * z),
+            device_id_type=MESH,
+        )
+
+    def pair_copy(it, c):
+        return pltpu.make_async_remote_copy(
+            src_ref=part.at[it, pl.ds(pl.multiple_of((1 - h) * n_z, n_z), n_z), :, pl.ds(c * cols, cols)],
+            dst_ref=pair_in.at[it, :, :, pl.ds(c * cols, cols)],
+            send_sem=pair_send.at[it, c],
+            recv_sem=pair_recv.at[it, c],
+            device_id=(ab, 2 * z + 1 - h),
+            device_id_type=MESH,
+        )
+
+    def red_copy(it, c, s):
+        to = lax.rem(z + s, n_z)
+        return pltpu.make_async_remote_copy(
+            src_ref=pair_out.at[it, to, :, pl.ds(c * cols, cols)],
+            dst_ref=arrived.at[it, s - 1, :, pl.ds(c * cols, cols)],
+            send_sem=red_send.at[it, c, s - 1],
+            recv_sem=red_recv.at[it, c, s - 1],
+            device_id=(ab, 2 * to + h),
+            device_id_type=MESH,
+        )
+
+    for it in range(ITERS):
+        packed[it] = state[...].astype(jnp.bfloat16)
+        for i in range(n_ab):
+            for k in range(2):
+                mine = (ab == i) & (cd == 2 * ab + k)
+
+                @pl.when(jnp.logical_not(mine))
+                def _():
+                    amp_copy(it, i, k).start()
+
+                @pl.when(mine)
+                def _():
+                    amp_local_copy(it, k).start()
+                    amp_local_copy(it, k).wait()
+        for j in range(n_cd):
+            @pl.when(jnp.logical_not((ab == z) & (cd == j)))
+            def _():
+                amp_arrival(it, j).wait_recv()
+
+        def reduce_chunk(c):
+            pair_copy(it, c).wait_recv()
+            at = pl.ds(c * cols, cols)
+            total = part[it, pl.ds(pl.multiple_of(h * n_z, n_z), n_z), :, at].astype(jnp.float32) + pair_in[
+                it, :, :, at
+            ].astype(jnp.float32)
+            pair_out[it, :, :, at] = total.astype(jnp.bfloat16)
+            for s in range(1, n_z):
+                red_copy(it, c, s).start()
+
+        for c in range(chunks):
+            value = jnp.dot(
+                amps[it], v_ref[:, c * cols:(c + 1) * cols], preferred_element_type=jnp.float32
+            ).astype(jnp.bfloat16)
+            for j in range(n_cd):
+                part[it, (j % 2) * n_z + j // 2, :, c * cols:(c + 1) * cols] = value[j * rows:(j + 1) * rows]
+            pair_copy(it, c).start()
+            if c > 0:
+                reduce_chunk(c - 1)
+        reduce_chunk(chunks - 1)
+        for c in range(chunks):
+            for s in range(1, n_z):
+                red_copy(it, c, s).wait_recv()
+            at = pl.ds(c * cols, cols)
+            total = pair_out[it, z, :, at].astype(jnp.float32)
+            for s in range(1, n_z):
+                total = total + arrived[it, s - 1, :, at].astype(jnp.float32)
+            out_ref[it, :, at] = total
+            if it + 1 < ITERS:
+                old = state[:, at]
+                den = den_ref[:, at]
+                state[:, at] = old - (sym_drv_ref[:, at] + den * old + total) / den
+    for it in range(ITERS):
+        for i in range(n_ab):
+            for k in range(2):
+                @pl.when(jnp.logical_not((ab == i) & (cd == 2 * ab + k)))
+                def _():
+                    amp_copy(it, i, k).wait_send()
+        for c in range(chunks):
+            pair_copy(it, c).wait_send()
+            for s in range(1, n_z):
+                red_copy(it, c, s).wait_send()
+
+
+def ladders(tiles, sym_amp, sym_drv, den, n_ab, n_cd):
+    rows, width = sym_amp.shape
+    depth = tiles.shape[0]
+    n_z = n_cd // 2
+    chunks = 4
+    vmem = pl.BlockSpec(memory_space=pltpu.VMEM)
+    dma = pltpu.SemaphoreType.DMA
+    return pl.pallas_call(
+        functools.partial(ladder_kernel, n_ab, n_cd, chunks),
+        out_shape=jax.ShapeDtypeStruct((ITERS, rows, width), jnp.float32),
+        in_specs=[vmem] * 4,
+        out_specs=vmem,
+        scratch_shapes=[
+            pltpu.VMEM((ITERS, n_cd * rows, depth), jnp.bfloat16),
+            pltpu.VMEM((ITERS, n_cd, rows, width), jnp.bfloat16),
+            pltpu.VMEM((ITERS, n_z, rows, width), jnp.bfloat16),
+            pltpu.VMEM((ITERS, n_z, rows, width), jnp.bfloat16),
+            pltpu.VMEM((ITERS, n_z - 1, rows, width), jnp.bfloat16),
+            pltpu.VMEM((rows, width), jnp.float32),
+            pltpu.VMEM((ITERS, rows, width), jnp.bfloat16),
+            dma((ITERS, n_ab, 2)),
+            dma((ITERS, n_cd)),
+            dma((ITERS,)),
+            dma((ITERS, chunks)),
+            dma((ITERS, chunks)),
+            dma((ITERS, chunks, n_z - 1)),
+            dma((ITERS, chunks, n_z - 1)),
+        ],
+        compiler_params=pltpu.CompilerParams(
+            collective_id=0, has_side_effects=True, vmem_limit_bytes=52 * 2**20
+        ),
+        cost_estimate=pl.CostEstimate(
+            flops=2 * ITERS * n_cd * rows * depth * width,
+            bytes_accessed=tiles.size * 2,
+            transcendentals=0,
+        ),
+    )(tiles, sym_amp, sym_drv, den)
+
+
+def local_ladder(factors, amplitudes, driving, occ_energy, vir_energy):
+    rows, a_local, virtuals = amplitudes.shape
+    aux_width = factors.shape[2]
+    d_local = factors.shape[1]
+    n_ab = lax.axis_size("ab")
+    n_cd = lax.axis_size("cd")
+    cd_index = lax.axis_index("cd")
+    ab_index = lax.axis_index("ab")
+    left = lax.all_gather(factors, "cd", axis=1, tiled=True).reshape(a_local * virtuals, aux_width)
+    right = lax.all_gather(factors.transpose(1, 0, 2), "ab", axis=1, tiled=True)
+    right = right.reshape(d_local * virtuals, aux_width)
+
+    both = jnp.concatenate([amplitudes, driving], axis=0)
+    swapped = lax.all_to_all(both, "ab", split_axis=2, concat_axis=1, tiled=True).transpose(0, 2, 1)
+    symmetric = (0.5 * (both + swapped)).reshape(2, rows, a_local * virtuals)
+
+    n_occ = occ_energy.shape[0]
+    row_ids = cd_index * rows + lax.iota(jnp.int32, rows)
+    orbitals = lax.iota(jnp.int32, n_occ)
+    first_hot = (row_ids[:, None] // n_occ == orbitals[None, :]).astype(jnp.float32)
+    second_hot = (row_ids[:, None] % n_occ == orbitals[None, :]).astype(jnp.float32)
+    occ_pair = jnp.sum((first_hot + second_hot) * occ_energy[None, :], axis=1)
+    vir_rows = lax.dynamic_slice_in_dim(vir_energy, ab_index * a_local, a_local)
+    denominator = vir_rows[None, :, None] + vir_energy[None, None, :] - occ_pair[:, None, None]
+
+    tiles = integral_tiles(left, right, virtuals, d_local)
+    sums = ladders(
+        tiles, symmetric[0], symmetric[1], denominator.reshape(rows, a_local * virtuals), n_ab, n_cd
+    ).reshape(ITERS, rows, a_local, virtuals)
+    current = amplitudes
+    residual = amplitudes
+    for step in range(ITERS):
+        residual = driving + denominator * current + sums[step]
+        current = current - residual / denominator
+    return (current, residual)
+
+
 def solution(mesh):
     placed = (P("ab", "cd", None), P("cd", "ab", None), P("cd", "ab", None), P(), P())
+
+    def local(factors, amplitudes, driving, occ_energy, vir_energy):
+        rows, a_local, virtuals = amplitudes.shape
+        paired = a_local == 2 * factors.shape[1] and mesh.shape["cd"] == 2 * mesh.shape["ab"]
+        aligned = rows % 16 == 0 and virtuals % 128 == 0 and a_local % 8 == 0
+        form = local_ladder if paired and aligned else local_general
+        return form(factors, amplitudes, driving, occ_energy, vir_energy)
+
     return jax.shard_map(
         local,
         mesh=mesh,

time: 560 us -> 528 us (0.943); the launches traced: 550 us -> 528 us
  Pallas kernels: 0 us -> 258 us
  waiting for transfers between devices: 351 us -> 200 us
  matrix products: 66.7 us -> 0 us
  blocking collectives: 33.4 us -> 0 us
  local copies, waits for them, and re-layouts: 67.4 us -> 39.9 us
    pallas_call x0 -> x2, Pallas kernels: none -> 258 us  [the longest x1 215 us: ladders(): pl.pallas_call(functools.partial(ladder_kernel, n_ab, n_cd, chunks), out_...]
    all_gather x4 -> x2, waiting for transfers between devices: 249 us -> 175 us  [the longest x1 140 us: local_ladder(): lax.all_gather(factors, 'cd', axis=1, tiled=True)]
    dot_general x3 -> x0, matrix products: 66.7 us -> none  [the longest x1 41.3 us: local(): lax.dot_general(left_flat, piece.reshape(count * d_local, aux_width), (((...]
    reduce_scatter x1 -> x0, waiting for transfers between devices: 47.7 us -> none  [local(): lax.psum_scatter(lax.dot_general(flat_amps, tiles, (((0,), (1,)), ((), ()...]
    unnamed x7 -> x2, waiting for transfers between devices: 47.5 us -> 1.37 us
    all_to_all x3 -> x0, blocking collectives: 33.4 us -> none  [the longest x2 21.9 us: local(): lax.all_to_all(rounded.transpose(2, 1, 0), 'cd', split_axis=0, concat_axi...]
    convert_element_type x1 -> x0, local copies, waits for them, and re-layouts: 22.4 us -> none  [local(): tiles = product.transpose(0, 2, 3, 1).reshape(a_local, count, d_local * v...]
    all_to_all x1, waiting for transfers between devices: 6.49 us -> 23.4 us  [local_ladder(): lax.all_to_all(both, 'ab', split_axis=2, concat_axis=1, tiled=True)]
  transfers between devices with their start and end apart: 7 -> 3, of which waited for: 6 -> 3; matrix products, arithmetic and copies ran while one was open for 12% -> 9% of each run, Pallas kernels for 0% -> 0%
where the time goes in v1:
time: 528 us
  Pallas kernels  258 us (49%)
  waiting for transfers between devices  200 us (38%)
  local copies, waits for them, and re-layouts  39.9 us (8%)
  between operations  14.2 us (3%)
  other arithmetic  11.5 us (2%)
    pallas_call x1, Pallas kernels, ladders(): pl.pallas_call(functools.partial(ladder_kernel, n_ab, n_cd, chunks), out_...  215 us
    all_gather x1, waiting for transfers between devices, local_ladder(): lax.all_gather(factors, 'cd', axis=1, tiled=True)  140 us
    pallas_call x1, Pallas kernels, integral_tiles(): pl.pallas_call(functools.partial(integral_kernel, virtuals, d_local), gri...  42.8 us
    all_gather x1, waiting for transfers between devices, local_ladder(): right = lax.all_gather(factors.transpose(1, 0, 2), 'ab', axis=1, tiled=True)  35.6 us
    all_to_all x1, waiting for transfers between devices, local_ladder(): lax.all_to_all(both, 'ab', split_axis=2, concat_axis=1, tiled=True)  23.4 us
    unnamed x19, local copies, waits for them, and re-layouts  14.3 us
    all_gather x1, local copies, waits for them, and re-layouts, local_ladder(): right = lax.all_gather(factors.transpose(1, 0, 2), 'ab', axis=1, tiled=True)  12.2 us
  transfers between devices with their start and end apart: 3, of which 3 were waited for; matrix products, arithmetic and copies ran while one was open for 9% of the time, Pallas kernels for 0%

profile of v1, /device:TPU:22, one launch (start us, length us, event | category | flops | bytes accessed | tf_op | source)
XLA Modules:
  0.0 527.9 jit_solution(16754691529667679464)
XLA Ops:
  7.2 0.0 all-gather.5.cloned.1.call-start
  7.2 0.0 copy-start.1
  7.2 0.7 all-gather.5.cloned.1.call-update
  7.9 0.0 copy-start.2
  7.9 0.0 all-gather.3.cloned.1.call-start
  8.0 0.7 all-gather.3.cloned.1.call-update
  8.7 0.0 copy-done.1
  8.7 1.9 copy.24
  10.6 0.0 copy-done.2
  10.6 2.9 copy.25
  13.5 3.5 fusion.9
  17.0 0.0 copy-start.4
  17.0 0.0 copy-start.5
  17.0 4.4 reshape.118
  21.4 4.7 all-to-all-start
  26.1 0.0 copy-done.4
  26.1 0.1 dynamic_slice.3
  26.2 0.0 copy-done.5
  26.2 0.2 multiply_reduce_fusion
  26.4 0.1 broadcast_add_fusion
  26.4 0.1 add.88
  26.6 0.1 broadcast_subtract_fusion.den_ref
  26.7 23.4 %all-to-all-done = f32[4,1,65536]{2,1,0:T(1,128)} async-done(((f32[4,1,65536]{2,1,0:T(1,128)}), f32[4,1,65536]{2,1,0:T(1,128)}, u32[]{:S(2)}, u32[]{:S(2)}) %all-to-all-start) | async-done | bytes 1048608 | tf_op jit(solution)/shard_map/all_to_all | solution.py:296
  50.1 0.5 broadcast.115
  50.6 5.7 %reduce = f32[4,65536]{1,0:T(4,128)} reduce(f32[4,1,65536]{2,1,0:T(1,128)} %all-to-all-done, f32[]{:T(128)} %broadcast.115), dimensions={1}, to_apply=%all_to_all.13.reduce_sub_computation | reduce | bytes 2097156 | tf_op jit(solution)/shard_map/all_to_all | solution.py:296
  56.3 3.5 reshape.119
  59.8 0.0 copy-start
  59.8 3.0 copy.27
  62.8 0.0 copy-done
  62.8 0.7 fusion
  63.5 2.1 fusion.8
  65.6 3.6 copy.29
  69.2 2.2 copy.28
  71.4 1.8 copy_bitcast_fusion
  73.2 35.6 %all-gather.5.cloned.1.call-done = bf16[16,128,2048]{2,0,1:T(8,128)(2,1)} async-done(((bf16[16,32,2048]{2,0,1:T(8,128)(2,1)}), bf16[16,128,2048]{2,0,1:T(8,128)(2,1)}) %all-gather.5.cloned.1.call-update) | async-done | bytes 8388624 | tf_op jit(solution)/shard_map/all_gather | solution.py:292
  108.8 12.2 %copy.23 = bf16[16,128,2048]{2,1,0:T(8,128)(2,1)} copy(bf16[16,128,2048]{2,0,1:T(8,128)(2,1)} %all-gather.5.cloned.1.call-done) | data formatting | bytes 16777216 | tf_op jit(solution)/shard_map/all_gather | solution.py:292
  121.1 139.6 %all-gather.3.cloned.1.call-done = bf16[32,128,2048]{2,1,0:T(8,128)(2,1)} async-done(((bf16[32,16,2048]{2,1,0:T(8,128)(2,1)}), bf16[32,128,2048]{2,1,0:T(8,128)(2,1)}) %all-gather.3.cloned.1.call-update) | async-done | bytes 16777232 | tf_op jit(solution)/shard_map/all_gather | solution.py:291
  260.7 42.8 %shard_map.68.v_ref = bf16[2048,4096]{1,0:T(8,128)(2,1)} custom-call(bf16[4096,2048]{1,0:T(8,128)(2,1)} %bitcast.46, bf16[2048,2048]{1,0:T(8,128)(2,1)} %bitcast.40), custom_call_target="tpu_custom_call" | custom-call | flops 34359738368 | bytes 41943040 | tf_op jit(solution)/shard_map/pallas_call | solution.py:91
  303.5 214.8 %shard_map.69 = f32[2,32,4096]{2,1,0:T(8,128)} custom-call(bf16[2048,4096]{1,0:T(8,128)(2,1)} %shard_map.68.v_ref, f32[32,4096]{1,0:T(8,128)S(1)} %get-tuple-element.11.sym_amp_ref, f32[32,4096]{1,0:T(8,128)S(1)} %get-tuple-element.10.sym_drv_ref, f32[32,4096]{1,0:T(8,128)S(1)} %broadcast_subtract_fusion.den_ref), custom_call_target="tpu_custom_call" | custom-call | flops 8589934592 | bytes 16777216 | tf_op jit(solution)/shard_map/pallas_call | solution.py:251
  518.3 0.0 copy-start.3
  518.3 1.3 slice_bitcast_fusion
  519.6 0.1 copy.34
  519.7 0.1 copy.33
  519.8 0.0 copy-done.3
  519.8 1.3 fusion.6
  (2 shorter events, 0.0 us)
Async XLA Ops:
  7.2 101.6 %all-gather.5.cloned.1.call-start = ((), (), s32[]{:S(2)}) async-start(), calls=%async_computation.2 | async-start | bytes 10485760 | tf_op jit(solution)/shard_map/all_gather | solution.py:292
  7.2 1.5 copy-start.1
  7.9 2.7 copy-start.2
  7.9 252.8 %all-gather.3.cloned.1.call-start = ((), (), s32[]{:S(2)}) async-start(), calls=%async_computation.1 | async-start | bytes 18874368 | tf_op jit(solution)/shard_map/all_gather | solution.py:291
  17.0 9.1 %copy-start.4 = (f32[128]{0:T(128)S(1)}, f32[128]{0:T(128)}, u32[]{:S(2)}) copy-start(f32[128]{0:T(128)} %param.9) | copy-start | bytes 1540
  17.0 9.2 %copy-start.5 = (f32[32]{0:T(128)S(1)}, f32[32]{0:T(128)}, u32[]{:S(2)}) copy-start(f32[32]{0:T(128)} %param.8) | copy-start | bytes 388
  21.4 28.7 %all-to-all-start = ((f32[4,1,65536]{2,1,0:T(1,128)}), f32[4,1,65536]{2,1,0:T(1,128)}, u32[]{:S(2)}, u32[]{:S(2)}) async-start(f32[4,1,65536]{2,1,0:T(1,128)} %reshape.118), calls=%async_computation | async-start | bytes 2097152 | tf_op jit(solution)/shard_map/all_to_all | solution.py:296
  59.8 3.0 copy-start
  518.3 1.6 copy-start.3
Sparse Core Ops, SparseCore 0:
  9.8 98.9 all-gather.4
  110.4 150.2 all-gather.2

commit v2 on v1

--- a/solution.py
+++ b/solution.py
@@ -108,8 +108,8 @@
 
 def ladder_kernel(
     n_ab, n_cd, chunks, v_ref, sym_amp_ref, sym_drv_ref, den_ref, out_ref,
-    amps, part, pair_in, pair_out, arrived, state, packed,
-    amp_send, amp_recv, amp_local, pair_send, pair_recv, red_send, red_recv,
+    amps, part, pair_in, pair_out, arrived, state, relay,
+    layer_send, layer_recv, amp_send, amp_recv, amp_local, pair_send, pair_recv, red_send, red_recv,
 ):
     ab = lax.axis_index("ab")
     cd = lax.axis_index("cd")
@@ -130,26 +130,39 @@
 
     state[...] = sym_amp_ref[...]
 
-    def amp_copy(it, i, k):
-        return pltpu.make_async_remote_copy(
-            src_ref=packed.at[it, :, pl.ds(k * depth, depth)],
+    def layer_copy(it, s):
+        return pltpu.make_async_remote_copy(
+            src_ref=relay.at[it, ab],
+            dst_ref=relay.at[it, ab],
+            send_sem=layer_send.at[it, s - 1],
+            recv_sem=layer_recv.at[it, s - 1],
+            device_id=(lax.rem(ab + s, n_ab), cd),
+            device_id_type=MESH,
+        )
+
+    def slot(s):
+        return lax.rem(ab + n_ab - s, n_ab)
+
+    def amp_copy(it, s, k):
+        return pltpu.make_async_remote_copy(
+            src_ref=relay.at[it, slot(s), :, pl.ds(k * depth, depth)],
             dst_ref=amps.at[it, pl.ds(cd * rows, rows), :],
-            send_sem=amp_send.at[it, i, k],
+            send_sem=amp_send.at[it, s, k],
             recv_sem=amp_recv.at[it, cd],
-            device_id=(i, 2 * ab + k),
-            device_id_type=MESH,
-        )
-
-    def amp_local_copy(it, k):
+            device_id=(ab, 2 * slot(s) + k),
+            device_id_type=MESH,
+        )
+
+    def amp_local_copy(it, s, k):
         return pltpu.make_async_copy(
-            packed.at[it, :, pl.ds(k * depth, depth)],
+            relay.at[it, slot(s), :, pl.ds(k * depth, depth)],
             amps.at[it, pl.ds(cd * rows, rows), :],
             amp_local.at[it],
         )
 
     def amp_arrival(it, j):
         return pltpu.make_async_remote_copy(
-            src_ref=packed.at[it, :, pl.ds(0, depth)],
+            src_ref=relay.at[it, 0, :, pl.ds(0, depth)],
             dst_ref=amps.at[it, pl.ds(j * rows, rows), :],
             send_sem=amp_send.at[it, 0, 0],
             recv_sem=amp_recv.at[it, j],
@@ -179,21 +192,25 @@
         )
 
     for it in range(ITERS):
-        packed[it] = state[...].astype(jnp.bfloat16)
-        for i in range(n_ab):
+        relay[it, ab] = state[...].astype(jnp.bfloat16)
+        for s in range(1, n_ab):
+            layer_copy(it, s).start()
+        for s in range(n_ab):
+            if s > 0:
+                layer_copy(it, s).wait_recv()
             for k in range(2):
-                mine = (ab == i) & (cd == 2 * ab + k)
+                mine = cd == 2 * slot(s) + k
 
                 @pl.when(jnp.logical_not(mine))
                 def _():
-                    amp_copy(it, i, k).start()
+                    amp_copy(it, s, k).start()
 
                 @pl.when(mine)
                 def _():
-                    amp_local_copy(it, k).start()
-                    amp_local_copy(it, k).wait()
+                    amp_local_copy(it, s, k).start()
+                    amp_local_copy(it, s, k).wait()
         for j in range(n_cd):
-            @pl.when(jnp.logical_not((ab == z) & (cd == j)))
+            @pl.when(cd != j)
             def _():
                 amp_arrival(it, j).wait_recv()
 
@@ -230,11 +247,13 @@
                 den = den_ref[:, at]
                 state[:, at] = old - (sym_drv_ref[:, at] + den * old + total) / den
     for it in range(ITERS):
-        for i in range(n_ab):
+        for s in range(n_ab):
+            if s > 0:
+                layer_copy(it, s).wait_send()
             for k in range(2):
-                @pl.when(jnp.logical_not((ab == i) & (cd == 2 * ab + k)))
+                @pl.when(cd != 2 * slot(s) + k)
                 def _():
-                    amp_copy(it, i, k).wait_send()
+                    amp_copy(it, s, k).wait_send()
         for c in range(chunks):
             pair_copy(it, c).wait_send()
             for s in range(1, n_z):
@@ -260,7 +279,9 @@
             pltpu.VMEM((ITERS, n_z, rows, width), jnp.bfloat16),
             pltpu.VMEM((ITERS, n_z - 1, rows, width), jnp.bfloat16),
             pltpu.VMEM((rows, width), jnp.float32),
-            pltpu.VMEM((ITERS, rows, width), jnp.bfloat16),
+            pltpu.VMEM((ITERS, n_ab, rows, width), jnp.bfloat16),
+            dma((ITERS, n_ab - 1)),
+            dma((ITERS, n_ab - 1)),
             dma((ITERS, n_ab, 2)),
             dma((ITERS, n_cd)),
             dma((ITERS,)),
@@ -289,7 +310,11 @@
     cd_index = lax.axis_index("cd")
     ab_index = lax.axis_index("ab")
     left = lax.all_gather(factors, "cd", axis=1, tiled=True).reshape(a_local * virtuals, aux_width)
-    right = lax.all_gather(factors.transpose(1, 0, 2), "ab", axis=1, tiled=True)
+    own = factors.transpose(1, 0, 2)
+    right = jnp.zeros((d_local, virtuals, aux_width), factors.dtype)
+    for s in range(n_ab):
+        block = lax.ppermute(own, "ab", [(i, i ^ s) for i in range(n_ab)]) if s else own
+        right = lax.dynamic_update_slice_in_dim(right, block, (ab_index ^ s) * a_local, axis=1)
     right = right.reshape(d_local * virtuals, aux_width)
 
     both = jnp.concatenate([amplitudes, driving], axis=0)
@@ -323,6 +348,7 @@
     def local(factors, amplitudes, driving, occ_energy, vir_energy):
         rows, a_local, virtuals = amplitudes.shape
         paired = a_local == 2 * factors.shape[1] and mesh.shape["cd"] == 2 * mesh.shape["ab"]
+        paired = paired and mesh.shape["ab"] & (mesh.shape["ab"] - 1) == 0
         aligned = rows % 16 == 0 and virtuals % 128 == 0 and a_local % 8 == 0
         form = local_ladder if paired and aligned else local_general
         return form(factors, amplitudes, driving, occ_energy, vir_energy)

time: 528 us -> 342 us (0.65); the launches traced: 528 us -> 336 us
  waiting for transfers between devices: 200 us -> 87 us
  Pallas kernels: 258 us -> 166 us
  local copies, waits for them, and re-layouts: 39.9 us -> 48.4 us
    all_gather x1, waiting for transfers between devices: 140 us -> 12.3 us  [local_ladder(): lax.all_gather(factors, 'cd', axis=1, tiled=True)]
    pallas_call x1, Pallas kernels: 215 us -> 123 us  [ladders(): pl.pallas_call(functools.partial(ladder_kernel, n_ab, n_cd, chunks), out_...]
    all_to_all x1, waiting for transfers between devices: 23.4 us -> 74 us  [local_ladder(): lax.all_to_all(both, 'ab', split_axis=2, concat_axis=1, tiled=True)]
    all_gather x1 -> x0, waiting for transfers between devices: 35.6 us -> none  [local_ladder(): right = lax.all_gather(factors.transpose(1, 0, 2), 'ab', axis=1, tiled=True)]
    dynamic_update_slice x0 -> x4, local copies, waits for them, and re-layouts: none -> 16.5 us  [local_ladder(): lax.dynamic_update_slice_in_dim(right, block, (ab_index ^ s) * a_local, a...]
    all_gather x1 -> x0, local copies, waits for them, and re-layouts: 12.2 us -> none  [local_ladder(): right = lax.all_gather(factors.transpose(1, 0, 2), 'ab', axis=1, tiled=True)]
  transfers between devices with their start and end apart: 3 -> 5, of which waited for: 3 -> 2; matrix products, arithmetic and copies ran while one was open for 9% -> 17% of each run, Pallas kernels for 0% -> 0%
where the time goes in v2:
time: 342 us; the launch traced here: 336 us
  Pallas kernels  166 us (49%)
  waiting for transfers between devices  87 us (25%)
  local copies, waits for them, and re-layouts  48.4 us (14%)
  between operations  14.2 us (4%)
  other arithmetic  11.7 us (3%)
  starting transfers between devices  8.29 us (2%)
    pallas_call x1, Pallas kernels, ladders(): pl.pallas_call(functools.partial(ladder_kernel, n_ab, n_cd, chunks), out_...  123 us
    all_to_all x1, waiting for transfers between devices, local_ladder(): lax.all_to_all(both, 'ab', split_axis=2, concat_axis=1, tiled=True)  74 us
    pallas_call x1, Pallas kernels, integral_tiles(): pl.pallas_call(functools.partial(integral_kernel, virtuals, d_local), gri...  42.8 us
    dynamic_update_slice x4, local copies, waits for them, and re-layouts, local_ladder(): lax.dynamic_update_slice_in_dim(right, block, (ab_index ^ s) * a_local, a...  16.5 us
    unnamed x19, local copies, waits for them, and re-layouts  14.4 us
    all_gather x1, waiting for transfers between devices, local_ladder(): lax.all_gather(factors, 'cd', axis=1, tiled=True)  12.3 us
  transfers between devices with their start and end apart: 5, of which 2 were waited for; matrix products, arithmetic and copies ran while one was open for 17% of the time, Pallas kernels for 0%

profile of v2, /device:TPU:22, one launch (start us, length us, event | category | flops | bytes accessed | tf_op | source)
XLA Modules:
  0.0 335.6 jit_solution(12618915482289455732)
XLA Ops:
  7.2 0.0 copy-start.1
  7.2 0.0 copy-start.2
  7.2 0.0 all-gather.2.cloned.1.call-start
  7.2 0.7 all-gather.2.cloned.1.call-update
  7.9 0.6 collective-permute-start
  8.5 0.5 collective-permute-start.1
  9.0 2.4 collective-permute-start.2
  11.5 0.0 copy-done.1
  11.5 1.9 copy.36
  13.4 0.0 copy-done.2
  13.4 2.9 copy.37
  16.3 3.8 %fusion.9 = f32[128,32,64]{2,1,0:T(8,128)} fusion(f32[32,32,128]{0,1,2:T(8,128)} %copy.37, f32[32,32,128]{0,1,2:T(8,128)S(1)} %copy.36), kind=kLoop, calls=%fused_computation.34 | loop fusion | flops 262144 | bytes 2097152
  20.0 0.0 copy-start.4
  20.0 0.0 copy-start.5
  20.0 4.4 %reshape.118 = f32[4,1,65536]{2,1,0:T(1,128)} reshape(f32[128,32,64]{2,1,0:T(8,128)} %fusion.9) | data formatting | bytes 2097152
  24.4 4.7 %all-to-all-start = ((f32[4,1,65536]{2,1,0:T(1,128)}), f32[4,1,65536]{2,1,0:T(1,128)}, u32[]{:S(2)}, u32[]{:S(2)}) async-start(f32[4,1,65536]{2,1,0:T(1,128)} %reshape.118), calls=%async_computation | async-start | bytes 2097152 | tf_op jit(solution)/shard_map/all_to_all | solution.py:321
  29.1 0.0 copy-done.4
  29.2 0.1 dynamic_slice.3
  29.2 0.0 copy-done.5
  29.2 0.2 multiply_reduce_fusion
  29.4 0.1 add.101
  29.5 0.1 broadcast_subtract_fusion.den_ref
  29.7 0.1 broadcast_add_fusion
  29.8 4.3 %broadcast_in_dim.2 = bf16[16,128,2048]{2,1,0:T(8,128)(2,1)} broadcast(bf16[]{:T(256)} %constant.46.clone.1), dimensions={} | broadcast | bytes 8388610 | tf_op jit(solution)/shard_map/broadcast_in_dim | solution.py:314
  34.0 4.1 %copy_dynamic-update-slice_fusion.3 = bf16[16,128,2048]{2,1,0:T(8,128)(2,1)} fusion(bf16[16,128,2048]{2,1,0:T(8,128)(2,1)} %broadcast_in_dim.2, s32[]{:T(128)S(6)} %select_n.35, bf16[16,32,2048]{2,0,1:T(8,128)(2,1)} %bitcast.1), kind=kLoop, calls=%fused_computation.6 | loop fusion | bytes 4194308 | tf_op jit(solution)/shard_map/dynamic_update_slice | solution.py:317
  38.1 74.0 %all-to-all-done = f32[4,1,65536]{2,1,0:T(1,128)} async-done(((f32[4,1,65536]{2,1,0:T(1,128)}), f32[4,1,65536]{2,1,0:T(1,128)}, u32[]{:S(2)}, u32[]{:S(2)}) %all-to-all-start) | async-done | bytes 1048608 | tf_op jit(solution)/shard_map/all_to_all | solution.py:321
  112.1 0.5 broadcast.119
  112.6 5.6 %reduce = f32[4,65536]{1,0:T(4,128)} reduce(f32[4,1,65536]{2,1,0:T(1,128)} %all-to-all-done, f32[]{:T(128)} %broadcast.119), dimensions={1}, to_apply=%all_to_all.13.reduce_sub_computation | reduce | bytes 2097156 | tf_op jit(solution)/shard_map/all_to_all | solution.py:321
  118.2 3.7 %reshape.119 = f32[128,32,64]{2,1,0:T(8,128)} reshape(f32[4,65536]{1,0:T(4,128)} %reduce) | data formatting | bytes 2097152
  121.9 0.0 copy-start
  121.9 3.0 copy.39
  124.8 0.0 copy-done
  124.8 0.7 fusion
  125.6 2.1 fusion.8
  127.6 3.6 %copy.40 = f32[32,32,128]{2,1,0:T(8,128)} copy(f32[32,32,128]{0,1,2:T(8,128)} %get-tuple-element.5) | data formatting | bytes 1048576 | tf_op jit(solution)/shard_map/slice | solution.py:335
  131.2 2.2 copy.41
  133.4 1.8 copy_bitcast_fusion
  135.2 0.0 collective-permute-done
  135.2 4.3 %copy_dynamic-update-slice_fusion.2 = bf16[16,128,2048]{2,1,0:T(8,128)(2,1)} fusion(bf16[16,128,2048]{2,1,0:T(8,128)(2,1)} %copy_dynamic-update-slice_fusion.3, s32[]{:T(128)S(6)} %select_n.38, bf16[16,32,2048]{2,0,1:T(8,128)(2,1)} %collective-permute-done), kind=kLoop, calls=%fused_computation.5 | loop fusion | bytes 4194308 | tf_op jit(solution)/shard_map/dynamic_update_slice | solution.py:317
  139.5 0.0 collective-permute-done.1
  139.5 4.0 %copy_dynamic-update-slice_fusion.1 = bf16[16,128,2048]{2,1,0:T(8,128)(2,1)} fusion(bf16[16,128,2048]{2,1,0:T(8,128)(2,1)} %copy_dynamic-update-slice_fusion.2, s32[]{:T(128)S(6)} %select_n.39, bf16[16,32,2048]{2,0,1:T(8,128)(2,1)} %collective-permute-done.1), kind=kLoop, calls=%fused_computation.4 | loop fusion | bytes 4194308 | tf_op jit(solution)/shard_map/dynamic_update_slice | solution.py:317
  143.6 0.0 collective-permute-done.2
  143.6 4.1 %copy_dynamic-update-slice_fusion = bf16[16,128,2048]{2,1,0:T(8,128)(2,1)} fusion(bf16[16,128,2048]{2,1,0:T(8,128)(2,1)} %copy_dynamic-update-slice_fusion.1, s32[]{:T(128)S(6)} %select_n.40, bf16[16,32,2048]{2,0,1:T(8,128)(2,1)} %collective-permute-done.2), kind=kLoop, calls=%fused_computation.3 | loop fusion | bytes 4194308 | tf_op jit(solution)/shard_map/dynamic_update_slice | solution.py:317
  147.7 12.3 %all-gather.2.cloned.1.call-done = bf16[32,128,2048]{2,1,0:T(8,128)(2,1)} async-done(((bf16[32,16,2048]{2,1,0:T(8,128)(2,1)}), bf16[32,128,2048]{2,1,0:T(8,128)(2,1)}) %all-gather.2.cloned.1.call-update) | async-done | bytes 16777232 | tf_op jit(solution)/shard_map/all_gather | solution.py:312
  160.0 42.8 %shard_map.68.v_ref = bf16[2048,4096]{1,0:T(8,128)(2,1)} custom-call(bf16[4096,2048]{1,0:T(8,128)(2,1)} %bitcast.44, bf16[2048,2048]{1,0:T(8,128)(2,1)} %bitcast.2.right_ref), custom_call_target="tpu_custom_call" | custom-call | flops 34359738368 | bytes 41943040 | tf_op jit(solution)/shard_map/pallas_call | solution.py:91
  202.8 123.1 %shard_map.69 = f32[2,32,4096]{2,1,0:T(8,128)} custom-call(bf16[2048,4096]{1,0:T(8,128)(2,1)} %shard_map.68.v_ref, f32[32,4096]{1,0:T(8,128)S(1)} %get-tuple-element.11.sym_amp_ref, f32[32,4096]{1,0:T(8,128)S(1)} %get-tuple-element.10.sym_drv_ref, f32[32,4096]{1,0:T(8,128)S(1)} %broadcast_subtract_fusion.den_ref), custom_call_target="tpu_custom_call" | custom-call | flops 8589934592 | bytes 16777216 | tf_op jit(solution)/shard_map/pallas_call | solution.py:270
  325.9 0.0 copy-start.3
  326.0 1.3 slice_bitcast_fusion
  327.3 0.1 copy.45
  327.4 0.1 copy.46
  327.5 0.0 copy-done.3
  327.5 1.3 fusion.6
  (2 shorter events, 0.0 us)
Async XLA Ops:
  7.2 4.3 %copy-start.1 = (f32[32,32,128]{2,1,0:T(8,128)S(1)}, f32[32,32,128]{2,1,0:T(8,128)}, u32[]{:S(2)}) copy-start(f32[32,32,128]{2,1,0:T(8,128)} %param.6) | copy-start | bytes 1572868
  7.2 6.2 %copy-start.2 = (f32[32,32,128]{2,1,0:T(8,128)S(1)}, f32[32,32,128]{2,1,0:T(8,128)}, u32[]{:S(2)}) copy-start(f32[32,32,128]{2,1,0:T(8,128)} %param.7) | copy-start | bytes 1572868
  7.2 152.8 %all-gather.2.cloned.1.call-start = ((), (), s32[]{:S(2)}) async-start(), calls=%async_computation.1 | async-start | bytes 18874368 | tf_op jit(solution)/shard_map/all_gather | solution.py:312
  7.9 127.3 %collective-permute-start = (bf16[16,32,2048]{2,0,1:T(8,128)(2,1)}, bf16[16,32,2048]{2,0,1:T(8,128)(2,1)}, u32[]{:S(2)}, u32[]{:S(2)}) collective-permute-start(bf16[16,32,2048]{2,0,1:T(8,128)(2,1)} %bitcast.1), channel_id=1, source_target_pairs={{0,8},{8,0},{16,24},{24,16},{1,9},{9,1},{17,25},{25,17},{2,10},{10... | collective-permute-start | bytes 6291464 | tf_op jit(solution)/shard_map/ppermute | solution.py:316
  8.5 131.0 %collective-permute-start.1 = (bf16[16,32,2048]{2,0,1:T(8,128)(2,1)}, bf16[16,32,2048]{2,0,1:T(8,128)(2,1)}, u32[]{:S(2)}, u32[]{:S(2)}) collective-permute-start(bf16[16,32,2048]{2,0,1:T(8,128)(2,1)} %bitcast.1), channel_id=1, source_target_pairs={{0,16},{8,24},{16,0},{24,8},{1,17},{9,25},{17,1},{25,9},{2,18},{10... | collective-permute-start | bytes 6291464 | tf_op jit(solution)/shard_map/ppermute | solution.py:316
  9.0 134.6 %collective-permute-start.2 = (bf16[16,32,2048]{2,0,1:T(8,128)(2,1)}, bf16[16,32,2048]{2,0,1:T(8,128)(2,1)}, u32[]{:S(2)}, u32[]{:S(2)}) collective-permute-start(bf16[16,32,2048]{2,0,1:T(8,128)(2,1)} %bitcast.1), channel_id=1, source_target_pairs={{0,24},{8,16},{16,8},{24,0},{1,25},{9,17},{17,9},{25,1},{2,26},{10... | collective-permute-start | bytes 6291464 | tf_op jit(solution)/shard_map/ppermute | solution.py:316
  20.0 9.1 %copy-start.4 = (f32[128]{0:T(128)S(1)}, f32[128]{0:T(128)}, u32[]{:S(2)}) copy-start(f32[128]{0:T(128)} %param.9) | copy-start | bytes 1540
  20.0 9.2 %copy-start.5 = (f32[32]{0:T(128)S(1)}, f32[32]{0:T(128)}, u32[]{:S(2)}) copy-start(f32[32]{0:T(128)} %param.8) | copy-start | bytes 388
  24.4 87.7 %all-to-all-start = ((f32[4,1,65536]{2,1,0:T(1,128)}), f32[4,1,65536]{2,1,0:T(1,128)}, u32[]{:S(2)}, u32[]{:S(2)}) async-start(f32[4,1,65536]{2,1,0:T(1,128)} %reshape.118), calls=%async_computation | async-start | bytes 2097152 | tf_op jit(solution)/shard_map/all_to_all | solution.py:321
  121.9 3.0 copy-start
  325.9 1.6 copy-start.3
Sparse Core Ops, SparseCore 0:
  9.6 150.2 all-gather.1
